TPU v7x, 128 devices: a whole 4x4x4 slice. The times are simulated.
128 devices in a mesh: ka: 8 (over z, x_hi), chol: 2 (over core), orb: 8 (over x_lo, y).
Axes of the slice: x: 4 (x_hi: 2, x_lo: 2; x = x_hi * 2 + x_lo), y: 4, z: 4, core: 2. Of those that a mesh axis runs over, the one named last changes fastest.
Arguments:
- chol_pairs: bfloat16 [2, 8, 2, 800, 104, 104], P(None, 'ka', None, 'chol', 'orb'), may hold values from -0.23925781 to 0.23925781
- green: bfloat16 [8, 4, 2, 104, 104], P('ka', None, None, 'orb'), may hold values from -0.625 to 0.625
- screening: float32 [2, 4, 800], P(None, None, 'chol'), may hold values from 0.25 to 4
Outputs:
- self_energy: float32 [8, 4, 2, 104, 104], P('ka', None, None, 'orb')
All inputs are finite; a program needn't handle non-finite values.
Results may differ from a plain program's by a relative error of at most 0.0028.
Values may be sent and summed in bfloat16 or wider, within the bound.
A program may use at most 256 MiB of HBM per device.

v0:
```python
import jax
import jax.numpy as jnp
from jax import lax
from jax.sharding import PartitionSpec as P


def shifted_2(block, axis, distance):
    devices = range(lax.axis_size(axis))
    route = [((i - distance) % len(devices), i) for i in devices]
    return lax.ppermute(block, axis, route)


def pair_image(pairs, shifted, weights):
    left_real = pairs[:, 0]
    left_imag = pairs[:, 1]
    green_real = shifted[:, :, 0]
    green_imag = shifted[:, :, 1]
    pattern = "kqim,ktml->ktqil"
    real_part = jnp.einsum(
        pattern, left_real, green_real, preferred_element_type=jnp.float32
    ) - jnp.einsum(pattern, left_imag, green_imag, preferred_element_type=jnp.float32)
    imag_part = jnp.einsum(
        pattern, left_real, green_imag, preferred_element_type=jnp.float32
    ) + jnp.einsum(pattern, left_imag, green_real, preferred_element_type=jnp.float32)
    factor = weights[None, :, :, None, None]
    return ((real_part * factor).astype(jnp.bfloat16), (imag_part * factor).astype(jnp.bfloat16))


def contract(images, row_block):
    pattern = "ktqil,kqjl->ktij"
    sum_real = 0.0
    sum_imag = 0.0
    for shift_index in range(len(images)):
        image_real, image_imag = images[shift_index]
        row_real = row_block[shift_index, :, 0]
        row_imag = row_block[shift_index, :, 1]
        sum_real = (
            sum_real
            + jnp.einsum(pattern, image_real, row_real, preferred_element_type=jnp.float32)
            + jnp.einsum(pattern, image_imag, row_imag, preferred_element_type=jnp.float32)
        )
        sum_imag = (
            sum_imag
            + jnp.einsum(pattern, image_imag, row_real, preferred_element_type=jnp.float32)
            - jnp.einsum(pattern, image_real, row_imag, preferred_element_type=jnp.float32)
        )
    return -jnp.stack([sum_real, sum_imag], axis=2)


def body(chol_pairs, green, screening):
    whole_green = lax.all_gather(green, "orb", axis=3, tiled=True)
    kpoint_devices = lax.axis_size("ka")
    offsets = (1, kpoint_devices // 2)
    shifted = []
    for offset in offsets:
        shifted.append(shifted_2(whole_green, "ka", offset))
    images = [
        pair_image(chol_pairs[shift_index], shifted[shift_index], screening[shift_index])
        for shift_index in range(len(offsets))
    ]
    partial_sum = contract(images, lax.all_gather(chol_pairs, "orb", axis=4, tiled=True))
    return lax.psum(partial_sum, "chol")


def solution(mesh):
    placed = (
        P(None, "ka", None, "chol", "orb", None),
        P("ka", None, None, "orb", None),
        P(None, None, "chol"),
    )
    return jax.shard_map(
        body,
        mesh=mesh,
        in_specs=placed,
        out_specs=P("ka", None, None, "orb", None),
        check_vma=False,
    )
```

profile of v0, /device:TPU:1, one launch (start us, length us, event | category | flops | bytes accessed | tf_op | source)
XLA Modules:
  0.0 557.6 jit_solution(12275297928725086628)
XLA Ops:
  6.5 0.0 copy-start.1
  6.5 0.0 all-gather.2.cloned.1.call-start
  6.5 5.3 copy.17
  11.9 0.0 all-gather.2.cloned.1.call-update
  11.9 0.0 copy-done.1
  11.9 0.0 copy-start.2
  11.9 25.4 %all_gather.6 = bf16[1,4,2,104,104]{4,1,2,0,3:T(4,128)(2,1)S(1)} all-gather(bf16[1,4,2,13,104]{4,1,2,0,3:T(4,128)(2,1)S(1)} %copy.15), channel_id=1, replica_groups=mesh['ka'=8,'chol'=2,'orb'=8] {'orb'}, dimensions={3}, use_global_device_ids=true | all-gather | bytes 194688 | tf_op jit(solution)/shard_map/all_gather | solution.py:51
  37.3 3.7 collective-permute-start.1
  41.0 2.4 collective-permute-start
  43.4 3.0 slice_bitcast_fusion.1
  46.4 0.0 copy-done.2
  46.4 0.0 copy-start
  46.5 0.0 collective-permute-done.1
  46.5 5.5 fusion.27
  52.0 0.0 copy-done
  52.0 1.5 fusion.26
  53.5 1.1 collective-permute-done
  54.6 5.5 fusion.25
  60.1 1.5 fusion.24
  61.6 7.0 %fusion.22 = bf16[4,400,13,104]{3,1,2,0:T(8,128)(2,1)} fusion(f32[4,104,400,13]{1,2,3,0:T(8,128)} %fusion.27, f32[4,400]{1,0:T(4,128)S(1)} %get-tuple-element.12, bf16[1,2,400,13,104]{4,2,3,1,0:T(8,128)(2,1)} %copy-done, bf16[1,4,2,104,104]{4,3,1,2,0:T(8,128)(2,1)S(1)} %collective-permute-done.1), kind=kOutput, calls=%fused_computation.30 | convolution fusion | flops 456435200 | bytes 16421888 | tf_op jit(solution)/shard_map/kqim,ktml->ktqil/dot_general | solution.py:19
  68.7 4.7 fusion.23
  73.4 6.6 %fusion.20 = bf16[4,400,13,104]{3,1,2,0:T(8,128)(2,1)} fusion(f32[4,104,400,13]{1,2,3,0:T(8,128)} %fusion.25, f32[4,400]{1,0:T(4,128)S(1)} %get-tuple-element.11, bf16[1,2,400,13,104]{4,2,3,1,0:T(8,128)(2,1)S(1)} %get-tuple-element.9, bf16[1,4,2,104,104]{4,3,1,2,0:T(8,128)(2,1)S(1)} %collective-permute-done), kind=kOutput, calls=%fused_computation.28 | convolution fusion | flops 456435200 | bytes 14425088 | tf_op jit(solution)/shard_map/kqim,ktml->ktqil/dot_general | solution.py:19
  80.0 3.4 fusion.21
  83.4 350.4 %all-gather.2.cloned.1.call-done = bf16[2,1,2,400,104,104]{5,3,2,1,0,4:T(8,128)(2,1)} async-done(((bf16[2,1,2,400,13,104]{5,3,2,1,0,4:T(8,128)(2,1)}), bf16[2,1,2,400,104,104]{5,3,2,1,0,4:T(8,128)(2,1)}) %all-gather.2.cloned.1.call-update) | async-done | bytes 34611216 | tf_op jit(solution)/shard_map/all_gather | solution.py:61
  433.8 30.7 %fusion.76 = (bf16[1,1,1,400,104,104]{5,3,2,1,0,4:T(8,128)(2,1)}, bf16[1,1,1,400,104,104]{5,3,2,1,0,4:T(8,128)(2,1)}, bf16[1,1,1,400,104,104]{5,3,2,1,0,4:T(8,128)(2,1)}, bf16[1,1,1,400,104,104]{5,3,2,1,0,4:T(8,128)(2,1)}) fusion(bf16[2,1,2,400,104,104]{5,3,2,1,0,4:T(8,128)(2,1)} %all-gather.2.cloned.1.call-done), kind=kLoop, calls=%fused_computation.65 | loop fusion | bytes 69222400 | tf_op jit(solution)/shard_map/slice | solution.py:35
  464.5 9.6 %fusion.31 = f32[4,13,104]{2,1,0:T(8,128)S(1)} fusion(bf16[1,1,1,400,104,104]{5,3,2,1,0,4:T(8,128)(2,1)} %get-tuple-element.8, bf16[4,400,13,104]{3,1,2,0:T(8,128)(2,1)} %fusion.22), kind=kOutput, calls=%fused_computation.43 | convolution fusion | flops 449945600 | bytes 13000832 | tf_op jit(solution)/shard_map/ktqil,kqjl->ktij/dot_general | solution.py:45
  474.1 9.6 %fusion.28 = f32[4,13,104]{2,1,0:T(8,128)S(1)} fusion(bf16[1,1,1,400,104,104]{5,3,2,1,0,4:T(8,128)(2,1)} %get-tuple-element.8, bf16[4,400,13,104]{3,1,2,0:T(8,128)(2,1)} %fusion.23), kind=kOutput, calls=%fused_computation.42 | convolution fusion | flops 449945600 | bytes 13000832 | tf_op jit(solution)/shard_map/ktqil,kqjl->ktij/dot_general | solution.py:40
  483.7 0.0 slice-start
  483.7 9.7 %fusion.37 = f32[4,13,104]{2,1,0:T(8,128)S(1)} fusion(bf16[1,1,1,400,104,104]{5,3,2,1,0,4:T(8,128)(2,1)} %get-tuple-element.6, bf16[4,400,13,104]{3,1,2,0:T(8,128)(2,1)} %fusion.23), kind=kOutput, calls=%fused_computation.45 | convolution fusion | flops 449945600 | bytes 13000832 | tf_op jit(solution)/shard_map/ktqil,kqjl->ktij/dot_general | solution.py:44
  493.4 0.0 slice-start.1
  493.4 9.6 %fusion.34 = f32[4,13,104]{2,1,0:T(8,128)S(1)} fusion(bf16[1,1,1,400,104,104]{5,3,2,1,0,4:T(8,128)(2,1)} %get-tuple-element.6, bf16[4,400,13,104]{3,1,2,0:T(8,128)(2,1)} %fusion.22), kind=kOutput, calls=%fused_computation.44 | convolution fusion | flops 449945600 | bytes 13000832 | tf_op jit(solution)/shard_map/ktqil,kqjl->ktij/dot_general | solution.py:39
  503.0 0.0 slice-done
  503.1 0.0 slice-done.1
  503.1 12.2 %fusion.43 = f32[4,13,104]{2,1,0:T(8,128)S(1)} fusion(bf16[1,1,1,400,104,104]{5,3,2,1,0,4:T(8,128)(2,1)} %get-tuple-element.7, bf16[4,400,13,104]{3,1,2,0:T(8,128)(2,1)S(1)} %bitcast.205), kind=kOutput, calls=%fused_computation.47 | convolution fusion | flops 449945600 | bytes 13000832 | tf_op jit(solution)/shard_map/ktqil,kqjl->ktij/dot_general | solution.py:45
  515.2 9.6 %fusion.40 = f32[4,13,104]{2,1,0:T(8,128)S(1)} fusion(bf16[1,1,1,400,104,104]{5,3,2,1,0,4:T(8,128)(2,1)} %get-tuple-element.7, bf16[4,400,13,104]{3,1,2,0:T(8,128)(2,1)} %fusion.21), kind=kOutput, calls=%fused_computation.46 | convolution fusion | flops 449945600 | bytes 13000832 | tf_op jit(solution)/shard_map/ktqil,kqjl->ktij/dot_general | solution.py:40
  524.8 9.6 %fusion.61 = f32[1,4,1,13,104]{4,3,1,2,0:T(8,128)S(1)} fusion(f32[4,13,104]{2,1,0:T(8,128)S(1)} %fusion.31, f32[4,13,104]{2,1,0:T(8,128)S(1)} %fusion.37, f32[4,13,104]{2,1,0:T(8,128)S(1)} %fusion.43, bf16[1,1,1,400,104,104]{5,3,2,1,0,4:T(8,128)(2,1)} %get-tuple-element.5, bf16[4,400,13,104]{3,1,2,0:T(8,128)(2,1)} %fusion.21), kind=kOutput, calls=%fused_computation.53 | convolution fusion | flops 449961824 | bytes 13065728 | tf_op jit(solution)/shard_map/ktqil,kqjl->ktij/dot_general | solution.py:44
  534.4 11.5 %fusion.73 = f32[1,4,1,13,104]{4,3,1,2,0:T(8,128)S(1)} fusion(f32[4,13,104]{2,1,0:T(8,128)S(1)} %fusion.28, f32[4,13,104]{2,1,0:T(8,128)S(1)} %fusion.34, f32[4,13,104]{2,1,0:T(8,128)S(1)} %fusion.40, bf16[1,1,1,400,104,104]{5,3,2,1,0,4:T(8,128)(2,1)} %get-tuple-element.5, bf16[4,400,13,104]{3,1,2,0:T(8,128)(2,1)S(1)} %bitcast.205), kind=kOutput, calls=%fused_computation.57 | convolution fusion | flops 449961824 | bytes 13065728 | tf_op jit(solution)/shard_map/ktqil,kqjl->ktij/dot_general | solution.py:39
  545.9 3.9 psum.7
  549.8 0.7 copy.31
  (5 shorter events, 0.1 us)
Async XLA Ops:
  6.5 5.3 copy-start.1
  6.5 427.3 %all-gather.2.cloned.1.call-start = ((), (), s32[]{:S(2)}) async-start(), calls=%async_computation | async-start | bytes 47923200 | tf_op jit(solution)/shard_map/all_gather | solution.py:61
  11.9 34.5 %copy-start.2 = (f32[2,4,400]{2,1,0:T(4,128)S(1)}, f32[2,4,400]{2,1,0:T(4,128)}, u32[]{:S(2)}) copy-start(f32[2,4,400]{2,1,0:T(4,128)} %param.5) | copy-start | bytes 38404
  37.3 9.1 %collective-permute-start.1 = (bf16[1,4,2,104,104]{4,3,1,2,0:T(8,128)(2,1)S(1)}, bf16[1,4,2,104,104]{4,3,1,2,0:T(8,128)(2,1)S(1)}, u32[]{:S(2)}, u32[]{:S(2)}) collective-permute-start(bf16[1,4,2,104,104]{4,3,1,2,0:T(8,128)(2,1)S(1)} %copy.16), channel_id=1, source_target_pairs={{64,0},{80,16},{96,32},{112,48},{0,64},{16,80},{32,96},{48,112},{6... | collective-permute-start | bytes 519176 | tf_op jit(solution)/shard_map/ppermute | solution.py:10
  41.0 13.6 %collective-permute-start = (bf16[1,4,2,104,104]{4,3,1,2,0:T(8,128)(2,1)S(1)}, bf16[1,4,2,104,104]{4,3,1,2,0:T(8,128)(2,1)S(1)}, u32[]{:S(2)}, u32[]{:S(2)}) collective-permute-start(bf16[1,4,2,104,104]{4,3,1,2,0:T(8,128)(2,1)S(1)} %copy.16), channel_id=1, source_target_pairs={{112,0},{0,16},{16,32},{32,48},{48,64},{64,80},{80,96},{96,112},{1... | collective-permute-start | bytes 519176 | tf_op jit(solution)/shard_map/ppermute | solution.py:10
  46.4 5.5 copy-start
  483.7 19.4 %slice-start = ((s8[5324800]{0:T(1024)(128)(4,1)}), s8[4194304]{0:T(1024)(128)(4,1)S(1)}, s32[]{:S(2)}) async-start(s8[5324800]{0:T(1024)(128)(4,1)} %bitcast.204), calls=%async_computation.1 | async-start | bytes 8388608
  493.4 9.7 %slice-start.1 = ((s8[5324800]{0:T(1024)(128)(4,1)}), s8[1130496]{0:T(1024)(128)(4,1)S(1)}, s32[]{:S(2)}) async-start(s8[5324800]{0:T(1024)(128)(4,1)} %bitcast.204), calls=%async_computation.2 | async-start | bytes 2260992
Sparse Core Ops, SparseCore 0:
  12.0 421.7 all-gather.1
where the time goes:
time: 566 us; the launch traced here: 558 us
  waiting for transfers between devices  352 us (62%)
  matrix products  117 us (21%)
  local copies, waits for them, and re-layouts  39.7 us (7%)
  blocking collectives  29.3 us (5%)
  between operations  13.8 us (2%)
  starting transfers between devices  6.13 us (1%)
    all_gather x1, waiting for transfers between devices, body(): lax.all_gather(chol_pairs, 'orb', axis=4, tiled=True)  350 us
    slice x1, local copies, waits for them, and re-layouts, contract(): row_real = row_block[shift_index, :, 0]  30.7 us
    all_gather x1, blocking collectives, body(): whole_green = lax.all_gather(green, 'orb', axis=3, tiled=True)  25.4 us
    dot_general x2, matrix products, contract(): jnp.einsum(pattern, image_real, row_imag, preferred_element_type=jnp.floa...  21.7 us
    dot_general x2, matrix products, contract(): jnp.einsum(pattern, image_real, row_real, preferred_element_type=jnp.floa...  21.1 us
    dot_general x2, matrix products, contract(): jnp.einsum(pattern, image_imag, row_real, preferred_element_type=jnp.floa...  19.3 us
    dot_general x2, matrix products, contract(): jnp.einsum(pattern, image_imag, row_imag, preferred_element_type=jnp.floa...  19.1 us
    dot_general x2, matrix products, pair_image(): jnp.einsum(pattern, left_real, green_real, preferred_element_type=jnp.flo...  13.6 us
  transfers between devices with their start and end apart: 3, of which 2 were waited for; matrix products, arithmetic and copies ran while one was open for 7% of the time, Pallas kernels for 0%

commit v1 on v0

v1 whole, which is shorter than its diff:
```python
import functools

import jax
import jax.numpy as jnp
from jax import lax
from jax.experimental import pallas as pl
from jax.experimental.pallas import tpu as pltpu
from jax.sharding import PartitionSpec as P

MESH = pl.DeviceIdType.MESH
BF16 = jnp.bfloat16
F32 = jnp.float32

ORB = 8
ROWS = 13
NORB = 104
PADDED = 112
TAUS = 4
VEC = 16
PER_Q = 25
SLOTS = 6
PLANES = 2 * ROWS
KEPT = 22
SPARE = 128 - NORB
PIECES = 5


def pad_lanes(x):
    return jnp.concatenate([x, jnp.zeros((x.shape[0], 128 - x.shape[1]), x.dtype)], axis=1)


def kernel(
    chol_ref, green_ref, screen_ref, out_ref,
    send, recv, extra, flat, image, rhs, weights, perm, total,
    green_in, green_all, half_in, piece, gathered, result, result_in,
    green_send, green_recv, gather_send, gather_recv, swap_send, swap_recv,
    pair_send, pair_recv, half_send, half_recv, piece_send, piece_recv, out_send, out_recv,
):
    k = lax.axis_index("ka")
    core = lax.axis_index("chol")
    me = lax.axis_index("orb")
    shift = 1 + 3 * core
    source_of = lax.rem(k + 8 - shift, 8)
    target_of = lax.rem(k + shift, 8)
    other = 1 - core

    def peer(d):
        dx, dy = d // 4, d % 4
        x = lax.rem(me // 4 + dx, 2)
        y = lax.rem(lax.rem(me, 4) + dy, 4)
        return x * 4 + y

    barrier = pltpu.get_barrier_semaphore()

    def greet(device):
        pl.semaphore_signal(barrier, inc=1, device_id=device, device_id_type=MESH)

    greet((source_of, core, me))
    greet((target_of, core, me))
    greet((k, other, me))
    for d in range(1, ORB):
        greet((k, core, peer(d)))
    pl.semaphore_wait(barrier, ORB + 2)

    shift_copy = pltpu.make_async_remote_copy(
        src_ref=green_ref, dst_ref=green_in, send_sem=green_send, recv_sem=green_recv,
        device_id=(target_of, core, me), device_id_type=MESH)
    shift_copy.start()

    row = lax.broadcasted_iota(jnp.int32, (256, 256), 0)
    col = lax.broadcasted_iota(jnp.int32, (256, 256), 1)
    hit = (lax.div(row, 16) == lax.rem(col, 16)) & (lax.rem(row, 16) == lax.div(col, 16))
    perm[...] = jnp.where(hit, 1.0, 0.0).astype(BF16)
    weights[...] = jnp.zeros_like(weights)
    rhs[...] = jnp.zeros_like(rhs)
    total[...] = jnp.zeros_like(total)

    shift_copy.wait()
    gather_copies = []
    for d in range(1, ORB):
        copy = pltpu.make_async_remote_copy(
            src_ref=green_in, dst_ref=green_all.at[core, me], send_sem=gather_send,
            recv_sem=gather_recv, device_id=(k, core, peer(d)), device_id_type=MESH)
        copy.start()
        gather_copies.append(copy)
    green_all[core, me] = green_in[...]

    lane = lax.broadcasted_iota(jnp.int32, (VEC, 128), 1)

    def fold(group, put):
        q = lax.div(group, PER_Q)
        at = pl.multiple_of(lax.rem(group, PER_Q) * VEC, VEC)

        def plane(f):
            return pad_lanes(chol_ref[q, f // ROWS, f % ROWS, pl.ds(at, VEC), :].astype(F32))

        for e in range(PLANES - KEPT):
            riding = plane(KEPT + e)
            for p in range(PIECES):
                f = PIECES * e + p
                moved = pltpu.roll(riding, (NORB - SPARE * p) % 128, 1)
                put(f, jnp.where(lane < NORB, plane(f), moved).astype(BF16))
        for f in range(PIECES * (PLANES - KEPT), KEPT):
            put(f, plane(f).astype(BF16))

    def fold_send(slot, group, to):
        def put(f, value):
            send[group, f] = value

        fold(group, put)
        pltpu.make_async_remote_copy(
            src_ref=send.at[group], dst_ref=recv.at[slot, me], send_sem=pair_send.at[slot],
            recv_sem=pair_recv.at[slot], device_id=(k, core, to), device_id_type=MESH).start()

    def fold_own(slot, group):
        def put(f, value):
            recv[slot, me, f] = value

        fold(group, put)

    def send_slot(slot, _):
        def send_one(d, _):
            to = peer(d)
            fold_send(slot, to * SLOTS + slot, to)
            return 0

        lax.fori_loop(1, ORB, send_one, 0)
        fold_own(slot, me * SLOTS + slot)
        return 0

    lax.fori_loop(0, SLOTS, send_slot, 0)

    first, second = 2 * core, 6 - 2 * core
    for number, to in ((0, first), (1, second)):
        left_over = ORB * SLOTS + number

        @pl.when(me != to)
        def _(to=to, left_over=left_over):
            fold_send(SLOTS, left_over, to)

        @pl.when(me == to)
        def _(to=to, left_over=left_over):
            fold_own(SLOTS, left_over)

    def wait_bytes(ref, sem):
        pltpu.make_async_copy(ref, ref, sem).wait()

    wait_bytes(green_all.at[core, pl.ds(0, ORB - 1)], gather_recv)
    swap = pltpu.make_async_remote_copy(
        src_ref=green_all.at[core], dst_ref=green_all.at[core], send_sem=swap_send,
        recv_sem=swap_recv, device_id=(k, other, me), device_id_type=MESH)
    swap.start()
    swap.wait()

    for q in range(2):
        for t in range(TAUS):
            parts = []
            for ri in range(2):
                blocks = [green_all[q, o, t, ri].astype(F32) for o in range(ORB)]
                parts.append(pad_lanes(jnp.concatenate(blocks, axis=0)))
            at = t * 256
            real, imag = parts
            weights[q, 0:NORB, at:at + 128] = real.astype(BF16)
            weights[q, 0:NORB, at + 128:at + 256] = imag.astype(BF16)
            weights[q, 128:128 + NORB, at:at + 128] = (-imag).astype(BF16)
            weights[q, 128:128 + NORB, at + 128:at + 256] = real.astype(BF16)

    def work(slot, group):
        q = lax.div(group, PER_Q)
        at = lax.rem(group, PER_Q) * VEC
        wait_bytes(recv.at[slot, pl.ds(0, ORB - 1)], pair_recv.at[slot])
        for o in range(ORB):
            for e in range(PLANES - KEPT):
                value = jnp.zeros((VEC, 128), F32)
                for p in range(PIECES):
                    carrier = recv[slot, o, PIECES * e + p].astype(F32)
                    back = pltpu.roll(carrier, (128 - NORB + SPARE * p) % 128, 1)
                    value = jnp.where(lane >= SPARE * p, back, value) if p else back
                extra[o, e] = value.astype(BF16)

        def plane(j, ri):
            o, r = j // ROWS, j % ROWS
            f = ri * ROWS + r
            return recv[slot, o, f] if f < KEPT else extra[o, f - KEPT]

        for jb in range(PADDED // 16):
            rows = [j for j in range(16 * jb, 16 * jb + 16) if j < NORB]
            both = jnp.concatenate(
                [jnp.concatenate([plane(j, ri) for j in rows], axis=0) for ri in range(2)], axis=1)
            turned = jnp.dot(perm[:, 0:16 * len(rows)], both, preferred_element_type=F32).astype(BF16)
            for v in range(VEC):
                tile = turned[16 * v:16 * v + 16]
                flat[v, 16 * jb:16 * jb + 16, :] = tile
                rhs[16 * jb:16 * jb + 16, 256 * v:256 * v + 256] = tile
                rhs[128 + 16 * jb:144 + 16 * jb, 256 * v:256 * v + 128] = -tile[:, 128:256]
                rhs[128 + 16 * jb:144 + 16 * jb, 256 * v + 128:256 * v + 256] = tile[:, 0:128]

        step = 4
        for v in range(0, VEC, step):
            left = flat[v:v + step].reshape(step * PADDED, 256)
            for t in range(TAUS):
                y = jnp.dot(left, weights[q, :, 256 * t:256 * t + 256], preferred_element_type=F32)
                for i in range(step):
                    scale = screen_ref[q, t, at + v + i]
                    image[PADDED * t:PADDED * t + PADDED, 256 * (v + i):256 * (v + i) + 256] = (
                        y[PADDED * i:PADDED * i + PADDED] * scale).astype(BF16)
        total[...] += lax.dot_general(
            image[...], rhs[...], (((1,), (1,)), ((), ())), preferred_element_type=F32)

    def work_slot(slot, _):
        work(slot, me * SLOTS + slot)
        return 0

    lax.fori_loop(0, SLOTS, work_slot, 0)
    has_more = (me == first) | (me == second)

    @pl.when(has_more)
    def _():
        work(SLOTS, ORB * SLOTS + jnp.where(me == first, 0, 1))

    half = 2 * PADDED
    swap_half = pltpu.make_async_remote_copy(
        src_ref=total.at[pl.ds(pl.multiple_of(other * half, half), half)], dst_ref=half_in,
        send_sem=half_send, recv_sem=half_recv, device_id=(k, other, me), device_id_type=MESH)
    swap_half.start()
    swap_half.wait()
    mine = total[pl.ds(pl.multiple_of(core * half, half), half), :] + half_in[...]
    for o in range(ORB):
        for t in range(2):
            for ri in range(2):
                at = t * PADDED + ROWS * o
                piece[o, t, ri, 0:ROWS] = -mine[at:at + ROWS, 128 * ri:128 * ri + 128]

    def send_piece(d, _):
        to = peer(d)
        pltpu.make_async_remote_copy(
            src_ref=piece.at[to], dst_ref=gathered.at[me], send_sem=piece_send,
            recv_sem=piece_recv, device_id=(k, core, to), device_id_type=MESH).start()
        return 0

    lax.fori_loop(1, ORB, send_piece, 0)
    gathered[me] = piece[me]
    wait_bytes(gathered.at[pl.ds(0, ORB - 1)], piece_recv)
    summed = gathered[0]
    for o in range(1, ORB):
        summed = summed + gathered[o]
    result[...] = summed
    hand_over = pltpu.make_async_remote_copy(
        src_ref=result, dst_ref=result_in, send_sem=out_send, recv_sem=out_recv,
        device_id=(k, other, me), device_id_type=MESH)
    hand_over.start()
    hand_over.wait()
    out_ref[pl.ds(2 * core, 2)] = result[:, :, 0:ROWS, 0:NORB]
    out_ref[pl.ds(2 * other, 2)] = result_in[:, :, 0:ROWS, 0:NORB]

    wait_bytes(green_all.at[core, pl.ds(0, ORB - 1)], gather_send)
    wait_bytes(piece.at[pl.ds(0, ORB - 1)], piece_send)

    def sent_slot(slot, _):
        wait_bytes(recv.at[slot, pl.ds(0, ORB - 1)], pair_send.at[slot])
        return 0

    lax.fori_loop(0, SLOTS, sent_slot, 0)

    @pl.when(has_more)
    def _():
        wait_bytes(recv.at[SLOTS, pl.ds(0, 1)], pair_send.at[SLOTS])

    @pl.when(jnp.logical_not(has_more))
    def _():
        wait_bytes(recv.at[SLOTS, pl.ds(0, 2)], pair_send.at[SLOTS])


def body(chol_pairs, green, screening):
    planes = jnp.transpose(chol_pairs[:, 0], (0, 1, 3, 2, 4))
    dma = pltpu.SemaphoreType.DMA
    out = pl.pallas_call(
        kernel,
        out_shape=jax.ShapeDtypeStruct((TAUS, 2, ROWS, NORB), F32),
        in_specs=[
            pl.BlockSpec(memory_space=pltpu.VMEM),
            pl.BlockSpec(memory_space=pltpu.VMEM),
            pl.BlockSpec(memory_space=pltpu.SMEM),
        ],
        out_specs=pl.BlockSpec(memory_space=pltpu.VMEM),
        scratch_shapes=[
            pltpu.VMEM((ORB * SLOTS + 2, KEPT, VEC, 128), BF16),
            pltpu.VMEM((SLOTS + 1, ORB, KEPT, VEC, 128), BF16),
            pltpu.VMEM((ORB, PLANES - KEPT, VEC, 128), BF16),
            pltpu.VMEM((VEC, PADDED, 256), BF16),
            pltpu.VMEM((TAUS * PADDED, VEC * 256), BF16),
            pltpu.VMEM((256, VEC * 256), BF16),
            pltpu.VMEM((2, 256, TAUS * 256), BF16),
            pltpu.VMEM((256, 256), BF16),
            pltpu.VMEM((TAUS * PADDED, 256), F32),
            pltpu.VMEM((TAUS, 2, ROWS, NORB), BF16),
            pltpu.VMEM((2, ORB, TAUS, 2, ROWS, NORB), BF16),
            pltpu.VMEM((2 * PADDED, 256), F32),
            pltpu.VMEM((ORB, 2, 2, 16, 128), F32),
            pltpu.VMEM((ORB, 2, 2, 16, 128), F32),
            pltpu.VMEM((2, 2, 16, 128), F32),
            pltpu.VMEM((2, 2, 16, 128), F32),
            dma, dma, dma, dma, dma, dma,
            dma((SLOTS + 1,)), dma((SLOTS + 1,)),
            dma, dma, dma, dma, dma, dma,
        ],
        compiler_params=pltpu.CompilerParams(
            collective_id=0, has_side_effects=True, vmem_limit_bytes=56 * 1024 * 1024),
        cost_estimate=pl.CostEstimate(
            flops=7_200_000_000, bytes_accessed=5_400_000, transcendentals=0),
    )(planes, green[0], screening)
    return out[None]


def solution(mesh):
    placed = (
        P(None, "ka", None, "chol", "orb", None),
        P("ka", None, None, "orb", None),
        P(None, None, "chol"),
    )
    return jax.shard_map(
        body,
        mesh=mesh,
        in_specs=placed,
        out_specs=P("ka", None, None, "orb", None),
        check_vma=False,
    )
```

time: 566 us -> 84.4 us (0.15); the launches traced: 558 us -> 84.2 us
  waiting for transfers between devices: 352 us -> 0 us
  matrix products: 117 us -> 0 us
  Pallas kernels: 0 us -> 81.4 us
  local copies, waits for them, and re-layouts: 39.7 us -> 2.85 us
  blocking collectives: 29.3 us -> 0 us
  between operations: 13.8 us -> 0.01 us
  starting transfers between devices: 6.13 us -> 0 us
    all_gather x1 -> x0, waiting for transfers between devices: 350 us -> none  [body(): lax.all_gather(chol_pairs, 'orb', axis=4, tiled=True)]
    dot_general x16 -> x0, matrix products: 117 us -> none  [the longest x2 21.7 us: contract(): jnp.einsum(pattern, image_real, row_imag, preferred_element_type=jnp.floa...]
    pallas_call x0 -> x1, Pallas kernels: none -> 81.4 us  [body(): pl.pallas_call(kernel, out_shape=jax.ShapeDtypeStruct((TAUS, 2, ROWS, NOR...]
    slice x1 -> x0, local copies, waits for them, and re-layouts: 30.7 us -> none  [contract(): row_real = row_block[shift_index, :, 0]]
    all_gather x1 -> x0, blocking collectives: 25.4 us -> none  [body(): whole_green = lax.all_gather(green, 'orb', axis=3, tiled=True)]
    ppermute x2 -> x0, starting transfers between devices: 6.13 us -> none  [shifted_2(): return lax.ppermute(block, axis, route)]
  transfers between devices with their start and end apart: 3 -> 0, of which waited for: 2 -> 0; matrix products, arithmetic and copies ran while one was open for 7% -> 0% of each run, Pallas kernels for 0% -> 0%
where the time goes in v1:
time: 84.4 us; the launch traced here: 84.2 us
  Pallas kernels  81.4 us (96%)
  local copies, waits for them, and re-layouts  2.85 us (3%)
    pallas_call x1, Pallas kernels, body(): pl.pallas_call(kernel, out_shape=jax.ShapeDtypeStruct((TAUS, 2, ROWS, NOR...  81.4 us

profile of v1, /device:TPU:1, one launch (start us, length us, event | category | flops | bytes accessed | tf_op | source)
XLA Modules:
  0.0 84.2 jit_solution(14132689561364423991)
XLA Ops:
  0.0 1.4 %copy.7 = bf16[1,4,2,13,104]{4,3,2,1,0:T(8,128)(2,1)} copy(bf16[1,4,2,13,104]{4,2,3,1,0:T(2,128)(2,1)} %param.4) | data formatting | bytes 43264 | tf_op args[1]
  1.4 81.4 %shard_map.37 = f32[4,2,13,104]{3,2,1,0:T(8,128)} custom-call(bf16[2,2,13,400,104]{4,3,2,1,0:T(8,128)(2,1)} %bitcast.9, bf16[4,2,13,104]{3,2,1,0:T(8,128)(2,1)} %bitcast.8, f32[2,4,400]{2,1,0:T(4,128)} %screen_ref.1), custom_call_target="tpu_custom_call" | custom-call | flops 7200000000 | bytes 5400000 | tf_op jit(solution)/shard_map/pallas_call | solution.py:277
  82.8 1.5 %copy.5 = f32[1,4,2,13,104]{4,2,3,1,0:T(2,128)} copy(f32[1,4,2,13,104]{4,3,2,1,0:T(8,128)} %bitcast.7) | data formatting | bytes 86528 | tf_op jit(solution)/shard_map/broadcast_in_dim | solution.py:312

commit v2 on v1

v2 whole, which is shorter than its diff:
```python
import functools

import jax
import jax.numpy as jnp
from jax import lax
from jax.experimental import pallas as pl
from jax.experimental.pallas import tpu as pltpu
from jax.sharding import PartitionSpec as P

MESH = pl.DeviceIdType.MESH
BF16 = jnp.bfloat16
F32 = jnp.float32

ORB = 8
ROWS = 13
NORB = 104
PADDED = 112
TAUS = 4
VEC = 16
PER_Q = 25
SLOTS = 6
PLANES = 2 * ROWS
KEPT = 22
SPARE = 128 - NORB
PIECES = 5


def pad_lanes(x):
    return jnp.concatenate([x, jnp.zeros((x.shape[0], 128 - x.shape[1]), x.dtype)], axis=1)


def kernel(
    chol_ref, green_ref, screen_ref, out_ref,
    loaded, send, recv, extra, flat, image, rhs, weights, perm, total, mine,
    green_mine, green_all, half_in, piece, gathered, result, result_in,
    load_sem, ready, gather_send, gather_recv, shift_send, shift_recv, swap_send, swap_recv,
    pair_send, pair_recv, half_send, half_recv, piece_send, piece_recv, out_send, out_recv,
):
    k = lax.axis_index("ka")
    core = lax.axis_index("chol")
    me = lax.axis_index("orb")
    other = 1 - core
    first, second = 2 * core, 6 - 2 * core
    has_more = (me == first) | (me == second)
    half = 2 * PADDED

    def peer(d):
        dx, dy = d // 4, d % 4
        x = lax.rem(me // 4 + dx, 2)
        y = lax.rem(lax.rem(me, 4) + dy, 4)
        return x * 4 + y

    def load(q):
        return pltpu.make_async_copy(chol_ref.at[q], loaded.at[q], load_sem.at[q])

    def wait_bytes(ref, sem):
        pltpu.make_async_copy(ref, ref, sem).wait()

    for q in range(2):
        load(q).start()

    barrier = pltpu.get_barrier_semaphore()

    def greet(device):
        pl.semaphore_signal(barrier, inc=1, device_id=device, device_id_type=MESH)

    near_to = (lax.rem(k + 1, 8), core, peer(4))
    near_from = (lax.rem(k + 7, 8), core, peer(4))
    far = (lax.rem(k + 4, 8), core, me)
    for d in range(1, ORB):
        greet((k, 0, peer(d)))

    @pl.when(core == 1)
    def _():
        greet((k, 0, me))
        greet(near_to)
        greet(near_from)
        greet(far)

    row = lax.broadcasted_iota(jnp.int32, (256, 256), 0)
    col = lax.broadcasted_iota(jnp.int32, (256, 256), 1)
    hit = (lax.div(row, 16) == lax.rem(col, 16)) & (lax.rem(row, 16) == lax.div(col, 16))
    perm[...] = jnp.where(hit, 1.0, 0.0).astype(BF16)
    for at in (PADDED, 128 + PADDED):
        rhs[at:at + 16, :] = jnp.zeros((16, VEC * 256), BF16)
    total[...] = jnp.zeros_like(total)
    weights[...] = jnp.zeros_like(weights)

    lane = lax.broadcasted_iota(jnp.int32, (VEC, 128), 1)

    def fold(group, put):
        q = lax.div(group, PER_Q)
        at = pl.multiple_of(lax.rem(group, PER_Q) * VEC, VEC)

        def plane(f):
            return pad_lanes(loaded[q, f // ROWS, f % ROWS, pl.ds(at, VEC), :].astype(F32))

        for e in range(PLANES - KEPT):
            riding = plane(KEPT + e)
            for p in range(PIECES):
                f = PIECES * e + p
                moved = pltpu.roll(riding, (NORB - SPARE * p) % 128, 1)
                put(f, jnp.where(lane < NORB, plane(f), moved).astype(BF16))
        for f in range(PIECES * (PLANES - KEPT), KEPT):
            put(f, plane(f).astype(BF16))

    def fold_to_send(group):
        def put(f, value):
            send[group, f] = value

        fold(group, put)

    def send_pairs(slot, group, to):
        pltpu.make_async_remote_copy(
            src_ref=send.at[group], dst_ref=recv.at[slot, me], send_sem=pair_send.at[slot],
            recv_sem=pair_recv.at[slot], device_id=(k, core, to), device_id_type=MESH).start()

    def fold_own(slot, group):
        def put(f, value):
            recv[slot, me, f] = value

        fold(group, put)

    for q in range(2):
        load(q).wait()

    def fold_first(d, _):
        fold_to_send(peer(d) * SLOTS)
        return 0

    lax.fori_loop(1, ORB, fold_first, 0)

    @pl.when(core == 0)
    def _():
        pl.semaphore_wait(barrier, 2 * ORB - 1)
        pl.semaphore_signal(ready, inc=1, device_id=(k, 1, me), device_id_type=MESH)

    @pl.when(core == 1)
    def _():
        pl.semaphore_wait(ready, 1)
        for d in range(1, ORB):
            pltpu.make_async_remote_copy(
                src_ref=green_ref, dst_ref=green_mine.at[me], send_sem=gather_send,
                recv_sem=gather_recv, device_id=(k, core, peer(d)), device_id_type=MESH).start()

    def send_first(d, _):
        to = peer(d)
        send_pairs(0, to * SLOTS, to)
        return 0

    lax.fori_loop(1, ORB, send_first, 0)
    fold_own(0, me * SLOTS)

    def send_slot(slot, _):
        def send_one(d, _):
            to = peer(d)
            group = to * SLOTS + slot
            fold_to_send(group)
            send_pairs(slot, group, to)
            return 0

        lax.fori_loop(1, ORB, send_one, 0)
        fold_own(slot, me * SLOTS + slot)
        return 0

    lax.fori_loop(1, SLOTS // 2, send_slot, 0)
    for number, to in ((0, first), (1, second)):
        left_over = ORB * SLOTS + number

        @pl.when(me != to)
        def _(to=to, left_over=left_over):
            fold_to_send(left_over)
            send_pairs(SLOTS, left_over, to)

        @pl.when(me == to)
        def _(left_over=left_over):
            fold_own(SLOTS, left_over)

    @pl.when(core == 1)
    def _():
        green_mine[me] = green_ref[...]
        wait_bytes(green_mine.at[pl.ds(0, ORB - 1)], gather_recv)
        pl.semaphore_wait(barrier, 3)
        for q, device in ((0, near_to), (1, far)):
            pltpu.make_async_remote_copy(
                src_ref=green_mine, dst_ref=green_all.at[q], send_sem=shift_send.at[q],
                recv_sem=shift_recv.at[q], device_id=device, device_id_type=MESH).start()

    lax.fori_loop(SLOTS // 2, SLOTS, send_slot, 0)

    hand_green = pltpu.make_async_remote_copy(
        src_ref=green_all, dst_ref=green_all, send_sem=swap_send,
        recv_sem=swap_recv, device_id=(k, 0, me), device_id_type=MESH)

    @pl.when(core == 1)
    def _():
        for q in range(2):
            wait_bytes(green_all.at[q], shift_recv.at[q])
        hand_green.start()

    @pl.when(core == 0)
    def _():
        hand_green.wait_recv()

    for q in range(2):
        for t in range(TAUS):
            parts = []
            for ri in range(2):
                blocks = [green_all[q, o, t, :, ri, :].astype(F32) for o in range(ORB)]
                parts.append(pad_lanes(jnp.concatenate(blocks, axis=0)))
            at = t * 256
            real, imag = parts
            weights[q, 0:NORB, at:at + 128] = real.astype(BF16)
            weights[q, 0:NORB, at + 128:at + 256] = imag.astype(BF16)
            weights[q, 128:128 + NORB, at:at + 128] = (-imag).astype(BF16)
            weights[q, 128:128 + NORB, at + 128:at + 256] = real.astype(BF16)

    swap_half = pltpu.make_async_remote_copy(
        src_ref=total.at[pl.ds(pl.multiple_of(other * half, half), half)], dst_ref=half_in,
        send_sem=half_send, recv_sem=half_recv, device_id=(k, other, me), device_id_type=MESH)

    def work(slot, group):
        q = lax.div(group, PER_Q)
        at = lax.rem(group, PER_Q) * VEC
        wait_bytes(recv.at[slot, pl.ds(0, ORB - 1)], pair_recv.at[slot])
        for o in range(ORB):
            for e in range(PLANES - KEPT):
                for p in range(PIECES):
                    carrier = recv[slot, o, PIECES * e + p].astype(F32)
                    back = pltpu.roll(carrier, (128 - NORB + SPARE * p) % 128, 1)
                    value = jnp.where(lane >= SPARE * p, back, value) if p else back
                extra[o, e] = value.astype(BF16)

        def plane(j, ri):
            o, r = j // ROWS, j % ROWS
            f = ri * ROWS + r
            return recv[slot, o, f] if f < KEPT else extra[o, f - KEPT]

        for jb in range(PADDED // 16):
            rows = [j for j in range(16 * jb, 16 * jb + 16) if j < NORB]
            both = jnp.concatenate(
                [jnp.concatenate([plane(j, ri) for j in rows], axis=0) for ri in range(2)], axis=1)
            turned = jnp.dot(perm[:, 0:16 * len(rows)], both, preferred_element_type=F32).astype(BF16)
            for v in range(VEC):
                tile = turned[16 * v:16 * v + 16]
                flat[v, 16 * jb:16 * jb + 16, :] = tile
                rhs[16 * jb:16 * jb + 16, 256 * v:256 * v + 256] = tile
                rhs[128 + 16 * jb:144 + 16 * jb, 256 * v:256 * v + 128] = -tile[:, 128:256]
                rhs[128 + 16 * jb:144 + 16 * jb, 256 * v + 128:256 * v + 256] = tile[:, 0:128]

        step = 4
        for v in range(0, VEC, step):
            left = flat[v:v + step].reshape(step * PADDED, 256)
            for t in range(TAUS):
                y = jnp.dot(left, weights[q, :, 256 * t:256 * t + 256], preferred_element_type=F32)
                for i in range(step):
                    scale = screen_ref[q, t, at + v + i]
                    image[PADDED * t:PADDED * t + PADDED, 256 * (v + i):256 * (v + i) + 256] = (
                        y[PADDED * i:PADDED * i + PADDED] * scale).astype(BF16)

        def add(rows):
            total[rows] += lax.dot_general(
                image[rows], rhs[...], (((1,), (1,)), ((), ())), preferred_element_type=F32)

        @pl.when(slot != SLOTS - 1)
        def _():
            add(slice(None))

        @pl.when(slot == SLOTS - 1)
        def _():
            add(pl.ds(pl.multiple_of(other * half, half), half))
            swap_half.start()
            add(pl.ds(pl.multiple_of(core * half, half), half))

    def work_at(position, _):
        left_over = position == SLOTS // 2
        slot = jnp.where(left_over, SLOTS, jnp.where(position < SLOTS // 2, position, position - 1))
        number = ORB * SLOTS + jnp.where(me == first, 0, 1)
        group = jnp.where(left_over, number, me * SLOTS + slot)

        @pl.when(jnp.logical_not(left_over) | has_more)
        def _():
            work(slot, group)

        return 0

    lax.fori_loop(0, SLOTS + 1, work_at, 0)

    swap_half.wait()
    mine[...] = -(total[pl.ds(pl.multiple_of(core * half, half), half), :] + half_in[...])
    for d in (4, 5, 7, 6, 1, 3, 2, 0):
        to = peer(d)
        for t in range(2):
            base = pl.multiple_of(lax.div(ROWS * to, 8) * 8, 8)
            around = mine[pl.ds(t * PADDED + base, 24), :]
            rows = pltpu.roll(around, 24 - (ROWS * to - base), 0)[0:ROWS]
            for ri in range(2):
                at = ROWS * (2 * t + ri)
                piece[d, at:at + ROWS] = rows[:, 128 * ri:128 * ri + 128]
        if d:
            pltpu.make_async_remote_copy(
                src_ref=piece.at[d], dst_ref=gathered.at[me], send_sem=piece_send,
                recv_sem=piece_recv, device_id=(k, core, to), device_id_type=MESH).start()
    gathered[me] = piece[0]
    wait_bytes(gathered.at[pl.ds(0, ORB - 1)], piece_recv)
    summed = gathered[0]
    for o in range(1, ORB):
        summed = summed + gathered[o]
    result[...] = summed
    hand_over = pltpu.make_async_remote_copy(
        src_ref=result, dst_ref=result_in, send_sem=out_send, recv_sem=out_recv,
        device_id=(k, other, me), device_id_type=MESH)
    hand_over.start()

    def put_out(which, ref):
        for t in range(2):
            for ri in range(2):
                at = ROWS * (2 * t + ri)
                out_ref[2 * which + t, :, ri, :] = ref[at:at + ROWS, 0:NORB]

    put_out(core, result)

    wait_bytes(piece.at[pl.ds(0, ORB - 1)], piece_send)

    def sent_slot(slot, _):
        wait_bytes(recv.at[slot, pl.ds(0, ORB - 1)], pair_send.at[slot])
        return 0

    lax.fori_loop(0, SLOTS, sent_slot, 0)

    @pl.when(has_more)
    def _():
        wait_bytes(recv.at[SLOTS, pl.ds(0, 1)], pair_send.at[SLOTS])

    @pl.when(jnp.logical_not(has_more))
    def _():
        wait_bytes(recv.at[SLOTS, pl.ds(0, 2)], pair_send.at[SLOTS])

    @pl.when(core == 1)
    def _():
        wait_bytes(green_mine.at[pl.ds(0, ORB - 1)], gather_send)
        for q in range(2):
            wait_bytes(green_mine, shift_send.at[q])
        hand_green.wait_send()

    hand_over.wait()
    put_out(other, result_in)


def body(chol_pairs, green, screening):
    planes = jnp.transpose(chol_pairs[:, 0], (0, 1, 3, 2, 4))
    dma = pltpu.SemaphoreType.DMA
    out = pl.pallas_call(
        kernel,
        out_shape=jax.ShapeDtypeStruct((TAUS, ROWS, 2, NORB), F32),
        in_specs=[
            pl.BlockSpec(memory_space=pl.ANY),
            pl.BlockSpec(memory_space=pltpu.VMEM),
            pl.BlockSpec(memory_space=pltpu.SMEM),
        ],
        out_specs=pl.BlockSpec(memory_space=pltpu.VMEM),
        scratch_shapes=[
            pltpu.VMEM((2, 2, ROWS, PER_Q * VEC, NORB), BF16),
            pltpu.VMEM((ORB * SLOTS + 2, KEPT, VEC, 128), BF16),
            pltpu.VMEM((SLOTS + 1, ORB, KEPT, VEC, 128), BF16),
            pltpu.VMEM((ORB, PLANES - KEPT, VEC, 128), BF16),
            pltpu.VMEM((VEC, PADDED, 256), BF16),
            pltpu.VMEM((TAUS * PADDED, VEC * 256), BF16),
            pltpu.VMEM((256, VEC * 256), BF16),
            pltpu.VMEM((2, 256, TAUS * 256), BF16),
            pltpu.VMEM((256, 256), BF16),
            pltpu.VMEM((TAUS * PADDED, 256), F32),
            pltpu.VMEM((2 * PADDED, 256), F32),
            pltpu.VMEM((ORB, TAUS, ROWS, 2, NORB), BF16),
            pltpu.VMEM((2, ORB, TAUS, ROWS, 2, NORB), BF16),
            pltpu.VMEM((2 * PADDED, 256), F32),
            pltpu.VMEM((ORB, 56, 128), F32),
            pltpu.VMEM((ORB, 56, 128), F32),
            pltpu.VMEM((56, 128), F32),
            pltpu.VMEM((56, 128), F32),
            dma((2,)), pltpu.SemaphoreType.REGULAR, dma, dma, dma((2,)), dma((2,)), dma, dma,
            dma((SLOTS + 1,)), dma((SLOTS + 1,)),
            dma, dma, dma, dma, dma, dma,
        ],
        compiler_params=pltpu.CompilerParams(
            collective_id=0, has_side_effects=True, vmem_limit_bytes=56 * 1024 * 1024),
        cost_estimate=pl.CostEstimate(
            flops=7_200_000_000, bytes_accessed=5_400_000, transcendentals=0),
    )(planes, jnp.transpose(green[0], (0, 2, 1, 3)), screening)
    return jnp.transpose(out, (0, 2, 1, 3))[None]


def solution(mesh):
    placed = (
        P(None, "ka", None, "chol", "orb", None),
        P("ka", None, None, "orb", None),
        P(None, None, "chol"),
    )
    return jax.shard_map(
        body,
        mesh=mesh,
        in_specs=placed,
        out_specs=P("ka", None, None, "orb", None),
        check_vma=False,
    )
```

time: 84.4 us -> 75.8 us (0.90)
  Pallas kernels: 81.4 us -> 74.1 us
  local copies, waits for them, and re-layouts: 2.85 us -> 1.44 us
    pallas_call x1, Pallas kernels: 81.4 us -> 74.1 us  [body(): pl.pallas_call(kernel, out_shape=jax.ShapeDtypeStruct((TAUS, ROWS, 2, NOR...]
    broadcast_in_dim x1 -> x0, local copies, waits for them, and re-layouts: 1.49 us -> none  [body(): return out[None]]
where the time goes in v2:
time: 75.8 us; the launch traced here: 75.5 us
  Pallas kernels  74.1 us (98%)
  local copies, waits for them, and re-layouts  1.44 us (2%)
    pallas_call x1, Pallas kernels, body(): pl.pallas_call(kernel, out_shape=jax.ShapeDtypeStruct((TAUS, ROWS, 2, NOR...  74.1 us

profile of v2, /device:TPU:1, one launch (start us, length us, event | category | flops | bytes accessed | tf_op | source)
XLA Modules:
  0.0 75.5 jit_solution(858974765088282815)
XLA Ops:
  0.0 74.1 %shard_map.37 = f32[4,13,2,104]{3,2,1,0:T(2,128)} custom-call(bf16[2,2,13,400,104]{4,3,2,1,0:T(8,128)(2,1)} %bitcast.10, bf16[4,13,2,104]{3,2,1,0:T(2,128)(2,1)} %bitcast.11, f32[2,4,400]{2,1,0:T(4,128)} %screen_ref.1), custom_call_target="tpu_custom_call" | custom-call | flops 7200000000 | bytes 5400000 | tf_op jit(solution)/shard_map/pallas_call | solution.py:353
  74.1 1.4 %copy.5 = f32[1,4,2,13,104]{4,2,3,1,0:T(2,128)} copy(f32[1,4,2,13,104]{4,2,3,1,0:T(2,128)} %bitcast.9) | data formatting | bytes 86528

commit v3 on v2

v3 whole, which is shorter than its diff:
```python
import functools

import jax
import jax.numpy as jnp
from jax import lax
from jax.experimental import pallas as pl
from jax.experimental.pallas import tpu as pltpu
from jax.sharding import PartitionSpec as P

MESH = pl.DeviceIdType.MESH
BF16 = jnp.bfloat16
F32 = jnp.float32

ORB = 8
ROWS = 13
NORB = 104
PADDED = 112
TAUS = 4
VEC = 16
PER_Q = 25
SLOTS = 6
WHOLE = SLOTS - 1
HALF = VEC // 2
PLANES = 2 * ROWS
KEPT = 22
LAST = 20
SPARE = 128 - NORB
PIECES = 5


def pad_lanes(x):
    return jnp.concatenate([x, jnp.zeros((x.shape[0], 128 - x.shape[1]), x.dtype)], axis=1)


def kernel(
    chol_ref, green_ref, screen_ref, out_ref,
    loaded, send, send_last, send_over, recv, recv_last, recv_over, bank, extra, flat, image, rhs, weights, perm, total, mine,
    green_mine, green_all, half_in, piece, gathered, result, result_in,
    load_sem, ready, gather_send, gather_recv, shift_send, shift_recv, swap_send, swap_recv,
    pair_send, pair_recv, last_send, last_recv, over_send, over_recv, half_send, half_recv, piece_send, piece_recv, out_send, out_recv,
):
    k = lax.axis_index("ka")
    core = lax.axis_index("chol")
    me = lax.axis_index("orb")
    other = 1 - core
    has_over = lax.rem(me // 4 + lax.rem(me, 4), 2) == core
    over_at = me // 2
    half = 2 * PADDED

    def peer(d):
        dx, dy = d // 4, d % 4
        x = lax.rem(me // 4 + dx, 2)
        y = lax.rem(lax.rem(me, 4) + dy, 4)
        return x * 4 + y

    def load(q):
        return pltpu.make_async_copy(chol_ref.at[q], loaded.at[q], load_sem.at[q])

    def wait_bytes(ref, sem):
        pltpu.make_async_copy(ref, ref, sem).wait()

    for q in range(2):
        load(q).start()

    barrier = pltpu.get_barrier_semaphore()

    def greet(device):
        pl.semaphore_signal(barrier, inc=1, device_id=device, device_id_type=MESH)

    near_to = (lax.rem(k + 1, 8), core, peer(4))
    near_from = (lax.rem(k + 7, 8), core, peer(4))
    far = (lax.rem(k + 4, 8), core, me)
    for d in range(1, ORB):
        greet((k, 0, peer(d)))

    @pl.when(core == 1)
    def _():
        greet((k, 0, me))
        greet(near_to)
        greet(near_from)
        greet(far)

    lane = lax.broadcasted_iota(jnp.int32, (VEC, 128), 1)

    def plane_of(group):
        q = lax.div(group, PER_Q)
        at = pl.multiple_of(lax.rem(group, PER_Q) * VEC, VEC)

        def plane(f):
            return pad_lanes(loaded[q, f // ROWS, f % ROWS, pl.ds(at, VEC), :].astype(F32))

        return plane

    def fold(plane, kept, put):
        for e in range(4):
            riding = plane(kept + e)
            for p in range(PIECES):
                f = PIECES * e + p
                moved = pltpu.roll(riding, (NORB - SPARE * p) % 128, 1)
                put(f, jnp.where(lane < NORB, plane(f), moved))

    def fold_slot(slot, to, put):
        plane, plane_last = plane_of(to * SLOTS + slot), plane_of(to * SLOTS + WHOLE)
        fold(plane, KEPT, put)
        for e in range(2):
            moved = pltpu.roll(plane_last(LAST + 4 + e), NORB - SPARE * slot, 1)
            put(LAST + e, jnp.where(lane < NORB, plane(LAST + e), moved))

    def halves(put):
        held = {}

        def put_plane(f, value):
            held[f] = value
            if f ^ 1 in held:
                a, b = held[f & ~1], held[f | 1]
                for h in range(2):
                    rows = slice(HALF * h, HALF * h + HALF)
                    put(h, f // 2, jnp.concatenate([a[rows], b[rows]], axis=0).astype(BF16))

        return put_plane

    def send_slot(slot, _):
        def send_one(d, _):
            to = peer(d)

            def put(f, value):
                send[slot, d, f] = value.astype(BF16)

            fold_slot(slot, to, put)
            pltpu.make_async_remote_copy(
                src_ref=send.at[slot, d], dst_ref=recv.at[slot, me], send_sem=pair_send.at[slot],
                recv_sem=pair_recv.at[slot], device_id=(k, core, to), device_id_type=MESH).start()
            return 0

        lax.fori_loop(1, ORB, send_one, 0)

        def put_own(f, value):
            recv[slot, me, f] = value.astype(BF16)

        fold_slot(slot, me, put_own)
        return 0

    for q in range(2):
        load(q).wait()

    @pl.when(core == 0)
    def _():
        pl.semaphore_wait(barrier, 2 * ORB - 1)
        pl.semaphore_signal(ready, inc=1, device_id=(k, 1, me), device_id_type=MESH)

    @pl.when(core == 1)
    def _():
        pl.semaphore_wait(ready, 1)
        for d in range(1, ORB):
            pltpu.make_async_remote_copy(
                src_ref=green_ref, dst_ref=green_mine.at[me], send_sem=gather_send,
                recv_sem=gather_recv, device_id=(k, core, peer(d)), device_id_type=MESH).start()

    send_slot(0, 0)

    row = lax.broadcasted_iota(jnp.int32, (256, 256), 0)
    col = lax.broadcasted_iota(jnp.int32, (256, 256), 1)
    hit = (lax.div(row, 16) == lax.rem(col, 16)) & (lax.rem(row, 16) == lax.div(col, 16))
    perm[...] = jnp.where(hit, 1.0, 0.0).astype(BF16)
    for at in (PADDED, 128 + PADDED):
        rhs[at:at + 16, :] = jnp.zeros((16, VEC * 256), BF16)
    total[...] = jnp.zeros_like(total)
    weights[...] = jnp.zeros_like(weights)

    send_slot(1, 0)

    @pl.when(core == 1)
    def _():
        green_mine[me] = green_ref[...]
        wait_bytes(green_mine.at[pl.ds(0, ORB - 1)], gather_recv)
        pl.semaphore_wait(barrier, 3)
        for q, device in ((0, near_to), (1, far)):
            pltpu.make_async_remote_copy(
                src_ref=green_mine, dst_ref=green_all.at[q], send_sem=shift_send.at[q],
                recv_sem=shift_recv.at[q], device_id=device, device_id_type=MESH).start()

    lax.fori_loop(2, WHOLE, send_slot, 0)

    for number in range(2):
        plane = plane_of(ORB * SLOTS + number)

        def put_over(h, n, value, number=number):
            send_over[2 * number + h, n] = value

        put = halves(put_over)
        fold(plane, KEPT, put)
        for f in range(LAST, KEPT):
            put(f, plane(f))
    for number in range(4):
        to = 2 * number + lax.rem(core + number // 2, 2)

        @pl.when(me != to)
        def _(number=number, to=to):
            pltpu.make_async_remote_copy(
                src_ref=send_over.at[number], dst_ref=recv_over.at[me], send_sem=over_send,
                recv_sem=over_recv, device_id=(k, core, to), device_id_type=MESH).start()

        @pl.when(me == to)
        def _(number=number):
            recv_over[me] = send_over[number]

    def fold_last(d, _):
        def put_last(h, n, value):
            send_last[h, d, n] = value

        fold(plane_of(peer(d) * SLOTS + WHOLE), LAST, halves(put_last))
        return 0

    def send_last_half(h):
        def send_one(d, _):
            pltpu.make_async_remote_copy(
                src_ref=send_last.at[h, d], dst_ref=recv_last.at[h, me], send_sem=last_send.at[h],
                recv_sem=last_recv.at[h], device_id=(k, core, peer(d)), device_id_type=MESH).start()
            return 0

        lax.fori_loop(1, ORB, send_one, 0)

    lax.fori_loop(0, ORB, fold_last, 0)
    for h in range(2):
        send_last_half(h)
        recv_last[h, me] = send_last[h, 0]

    hand_green = pltpu.make_async_remote_copy(
        src_ref=green_all, dst_ref=green_all, send_sem=swap_send,
        recv_sem=swap_recv, device_id=(k, 0, me), device_id_type=MESH)

    @pl.when(core == 1)
    def _():
        for q in range(2):
            wait_bytes(green_all.at[q], shift_recv.at[q])
        hand_green.start()

    @pl.when(core == 0)
    def _():
        hand_green.wait_recv()

    for q in range(2):
        for t in range(TAUS):
            parts = []
            for ri in range(2):
                blocks = [green_all[q, o, t, :, ri, :].astype(F32) for o in range(ORB)]
                parts.append(pad_lanes(jnp.concatenate(blocks, axis=0)))
            at = t * 256
            real, imag = parts
            weights[q, 0:NORB, at:at + 128] = real.astype(BF16)
            weights[q, 0:NORB, at + 128:at + 256] = imag.astype(BF16)
            weights[q, 128:128 + NORB, at:at + 128] = (-imag).astype(BF16)
            weights[q, 128:128 + NORB, at + 128:at + 256] = real.astype(BF16)

    swap_half = pltpu.make_async_remote_copy(
        src_ref=total.at[pl.ds(pl.multiple_of(other * half, half), half)], dst_ref=half_in,
        send_sem=half_send, recv_sem=half_recv, device_id=(k, other, me), device_id_type=MESH)

    def unfold(planes, kept, o, put):
        for e in range(4):
            for p in range(PIECES):
                carrier = planes(PIECES * e + p).astype(F32)
                back = pltpu.roll(carrier, SPARE + SPARE * p, 1)
                value = jnp.where(lane >= SPARE * p, back, value) if p else back
            put(e, value.astype(BF16))

    def turn(plane, vectors):
        for jb in range(PADDED // 16):
            rows = [j for j in range(16 * jb, 16 * jb + 16) if j < NORB]
            both = jnp.concatenate(
                [jnp.concatenate([plane(j // ROWS, ri * ROWS + j % ROWS) for j in rows], axis=0)
                 for ri in range(2)], axis=1)
            turned = jnp.dot(perm[0:16 * vectors, 0:16 * len(rows)], both,
                             preferred_element_type=F32).astype(BF16)
            for v in range(vectors):
                tile = turned[16 * v:16 * v + 16]
                flat[v, 16 * jb:16 * jb + 16, :] = tile
                rhs[16 * jb:16 * jb + 16, 256 * v:256 * v + 256] = tile
                rhs[128 + 16 * jb:144 + 16 * jb, 256 * v:256 * v + 128] = -tile[:, 128:256]
                rhs[128 + 16 * jb:144 + 16 * jb, 256 * v + 128:256 * v + 256] = tile[:, 0:128]

    def image_of(q, at, vectors):
        step = 4
        for v in range(0, vectors, step):
            left = flat[v:v + step].reshape(step * PADDED, 256)
            for t in range(TAUS):
                y = jnp.dot(left, weights[q, :, 256 * t:256 * t + 256], preferred_element_type=F32)
                for i in range(step):
                    scale = screen_ref[q, t, at + v + i]
                    image[PADDED * t:PADDED * t + PADDED, 256 * (v + i):256 * (v + i) + 256] = (
                        y[PADDED * i:PADDED * i + PADDED] * scale).astype(BF16)

    def add(rows, vectors):
        cols = slice(0, 256 * vectors)
        total[rows] += lax.dot_general(
            image[rows, cols], rhs[:, cols], (((1,), (1,)), ((), ())), preferred_element_type=F32)

    def work_whole(slot, _):
        group = me * SLOTS + slot
        wait_bytes(recv.at[slot, pl.ds(0, ORB - 1)], pair_recv.at[slot])
        for o in range(ORB):
            def put(e, value, o=o):
                extra[o, e] = value

            unfold(lambda f, o=o: recv[slot, o, f], KEPT, o, put)
        turn(lambda o, f: recv[slot, o, f] if f < KEPT else extra[o, f - KEPT], VEC)
        image_of(lax.div(group, PER_Q), lax.rem(group, PER_Q) * VEC, VEC)
        add(slice(None), VEC)
        return 0

    def turned_over(value):
        return jnp.concatenate([value[HALF:], value[:HALF]], axis=0)

    def unpack(tiles, kept):
        for o in range(ORB):
            for n in range(kept // 2):
                tile = tiles(o, n)
                bank[o, 2 * n] = tile
                bank[o, 2 * n + 1] = turned_over(tile.astype(F32)).astype(BF16)

            def put(e, value, o=o):
                bank[o, kept + e] = value

            unfold(lambda f, o=o: bank[o, f], kept, o, put)

    def work_half(position, _):
        h = jnp.where(position == 0, lax.rem(over_at, 2), position - 1)
        group = jnp.where(position == 0, ORB * SLOTS + over_at // 2, me * SLOTS + WHOLE)

        @pl.when(position == 0)
        def _():
            wait_bytes(recv_over.at[pl.ds(0, ORB - 1)], over_recv)
            unpack(lambda o, n: recv_over[o, n], KEPT)

        @pl.when(position != 0)
        def _():
            wait_bytes(recv_last.at[h, pl.ds(0, ORB - 1)], last_recv.at[h])
            unpack(lambda o, n: recv_last[h, o, n], LAST)
            for o in range(ORB):
                for e in range(2):
                    for p in range(PIECES):
                        back = pltpu.roll(recv[p, o, LAST + e].astype(F32), SPARE + SPARE * p, 1)
                        value = jnp.where(lane >= SPARE * p, back, value) if p else back
                    bank[o, LAST + 4 + e] = jnp.where(h == 1, turned_over(value), value).astype(BF16)

        turn(lambda o, f: bank[o, f], HALF)
        image_of(lax.div(group, PER_Q), lax.rem(group, PER_Q) * VEC + HALF * h, HALF)

        @pl.when(position != 2)
        def _():
            add(slice(None), HALF)

        @pl.when(position == 2)
        def _():
            add(pl.ds(pl.multiple_of(other * half, half), half), HALF)
            swap_half.start()
            add(pl.ds(pl.multiple_of(core * half, half), half), HALF)

        return 0

    lax.fori_loop(0, WHOLE, work_whole, 0)
    lax.fori_loop(jnp.where(has_over, 0, 1), 3, work_half, 0)

    swap_half.wait()
    mine[...] = -(total[pl.ds(pl.multiple_of(core * half, half), half), :] + half_in[...])
    for d in (4, 5, 7, 6, 1, 3, 2, 0):
        to = peer(d)
        for t in range(2):
            base = pl.multiple_of(lax.div(ROWS * to, 8) * 8, 8)
            around = mine[pl.ds(t * PADDED + base, 24), :]
            rows = pltpu.roll(around, 24 - (ROWS * to - base), 0)[0:ROWS]
            for ri in range(2):
                at = ROWS * (2 * t + ri)
                piece[d, at:at + ROWS] = rows[:, 128 * ri:128 * ri + 128]
        if d:
            pltpu.make_async_remote_copy(
                src_ref=piece.at[d], dst_ref=gathered.at[me], send_sem=piece_send,
                recv_sem=piece_recv, device_id=(k, core, to), device_id_type=MESH).start()
    gathered[me] = piece[0]
    wait_bytes(gathered.at[pl.ds(0, ORB - 1)], piece_recv)
    summed = gathered[0]
    for o in range(1, ORB):
        summed = summed + gathered[o]
    result[...] = summed
    hand_over = pltpu.make_async_remote_copy(
        src_ref=result, dst_ref=result_in, send_sem=out_send, recv_sem=out_recv,
        device_id=(k, other, me), device_id_type=MESH)
    hand_over.start()

    def put_out(which, ref):
        for t in range(2):
            for ri in range(2):
                at = ROWS * (2 * t + ri)
                out_ref[2 * which + t, :, ri, :] = ref[at:at + ROWS, 0:NORB]

    put_out(core, result)

    wait_bytes(piece.at[pl.ds(0, ORB - 1)], piece_send)

    def sent_slot(slot, _):
        wait_bytes(recv.at[slot, pl.ds(0, ORB - 1)], pair_send.at[slot])
        return 0

    lax.fori_loop(0, WHOLE, sent_slot, 0)
    for h in range(2):
        wait_bytes(recv_last.at[h, pl.ds(0, ORB - 1)], last_send.at[h])

    @pl.when(has_over)
    def _():
        wait_bytes(recv_over.at[pl.ds(0, 3)], over_send)

    @pl.when(jnp.logical_not(has_over))
    def _():
        wait_bytes(recv_over.at[pl.ds(0, 4)], over_send)

    @pl.when(core == 1)
    def _():
        wait_bytes(green_mine.at[pl.ds(0, ORB - 1)], gather_send)
        for q in range(2):
            wait_bytes(green_mine, shift_send.at[q])
        hand_green.wait_send()

    hand_over.wait()
    put_out(other, result_in)


def body(chol_pairs, green, screening):
    planes = jnp.transpose(chol_pairs[:, 0], (0, 1, 3, 2, 4))
    dma = pltpu.SemaphoreType.DMA
    out = pl.pallas_call(
        kernel,
        out_shape=pltpu.VMEM((TAUS, ROWS, 2, NORB), F32),
        in_specs=[
            pl.BlockSpec(memory_space=pl.ANY),
            pl.BlockSpec(memory_space=pltpu.VMEM),
            pl.BlockSpec(memory_space=pltpu.SMEM),
        ],
        out_specs=pl.BlockSpec(memory_space=pltpu.VMEM),
        scratch_shapes=[
            pltpu.VMEM((2, 2, ROWS, PER_Q * VEC, NORB), BF16),
            pltpu.VMEM((WHOLE, ORB, KEPT, VEC, 128), BF16),
            pltpu.VMEM((2, ORB, LAST // 2, VEC, 128), BF16),
            pltpu.VMEM((4, KEPT // 2, VEC, 128), BF16),
            pltpu.VMEM((WHOLE, ORB, KEPT, VEC, 128), BF16),
            pltpu.VMEM((2, ORB, LAST // 2, VEC, 128), BF16),
            pltpu.VMEM((ORB, KEPT // 2, VEC, 128), BF16),
            pltpu.VMEM((ORB, PLANES, VEC, 128), BF16),
            pltpu.VMEM((ORB, PLANES - KEPT, VEC, 128), BF16),
            pltpu.VMEM((VEC, PADDED, 256), BF16),
            pltpu.VMEM((TAUS * PADDED, VEC * 256), BF16),
            pltpu.VMEM((256, VEC * 256), BF16),
            pltpu.VMEM((2, 256, TAUS * 256), BF16),
            pltpu.VMEM((256, 256), BF16),
            pltpu.VMEM((TAUS * PADDED, 256), F32),
            pltpu.VMEM((2 * PADDED, 256), F32),
            pltpu.VMEM((ORB, TAUS, ROWS, 2, NORB), BF16),
            pltpu.VMEM((2, ORB, TAUS, ROWS, 2, NORB), BF16),
            pltpu.VMEM((2 * PADDED, 256), F32),
            pltpu.VMEM((ORB, 56, 128), F32),
            pltpu.VMEM((ORB, 56, 128), F32),
            pltpu.VMEM((56, 128), F32),
            pltpu.VMEM((56, 128), F32),
            dma((2,)), pltpu.SemaphoreType.REGULAR, dma, dma, dma((2,)), dma((2,)), dma, dma,
            dma((WHOLE,)), dma((WHOLE,)), dma((2,)), dma((2,)), dma, dma,
            dma, dma, dma, dma, dma, dma,
        ],
        compiler_params=pltpu.CompilerParams(
            collective_id=0, has_side_effects=True, vmem_limit_bytes=56 * 1024 * 1024),
        cost_estimate=pl.CostEstimate(
            flops=7_200_000_000, bytes_accessed=5_400_000, transcendentals=0),
    )(planes, jnp.transpose(green[0], (0, 2, 1, 3)), screening)
    return jnp.transpose(out, (0, 2, 1, 3))[None]


def solution(mesh):
    placed = (
        P(None, "ka", None, "chol", "orb", None),
        P("ka", None, None, "orb", None),
        P(None, None, "chol"),
    )
    return jax.shard_map(
        body,
        mesh=mesh,
        in_specs=placed,
        out_specs=P("ka", None, None, "orb", None),
        check_vma=False,
    )
```

time: 75.8 us -> 69.1 us (0.912)
  Pallas kernels: 74.1 us -> 68.3 us
  local copies, waits for them, and re-layouts: 1.44 us -> 0.62 us
    pallas_call x1, Pallas kernels: 74.1 us -> 68.3 us  [body(): pl.pallas_call(kernel, out_shape=pltpu.VMEM((TAUS, ROWS, 2, NORB), F32),...]
    unnamed x1, local copies, waits for them, and re-layouts: 1.44 us -> 0.62 us
where the time goes in v3:
time: 69.1 us; the launch traced here: 69 us
  Pallas kernels  68.3 us (99%)
    pallas_call x1, Pallas kernels, body(): pl.pallas_call(kernel, out_shape=pltpu.VMEM((TAUS, ROWS, 2, NORB), F32),...  68.3 us

profile of v3, /device:TPU:1, one launch (start us, length us, event | category | flops | bytes accessed | tf_op | source)
XLA Modules:
  0.0 69.0 jit_solution(5483942082033630848)
XLA Ops:
  0.0 68.3 %shard_map.37 = f32[4,13,2,104]{3,2,1,0:T(2,128)S(1)} custom-call(bf16[2,2,13,400,104]{4,3,2,1,0:T(8,128)(2,1)} %bitcast.10, bf16[4,13,2,104]{3,2,1,0:T(2,128)(2,1)} %bitcast.11, f32[2,4,400]{2,1,0:T(4,128)} %screen_ref.1), custom_call_target="tpu_custom_call" | custom-call | flops 7200000000 | bytes 5400000 | tf_op jit(solution)/shard_map/pallas_call | solution.py:430
  68.3 0.6 copy.5

commit v4 on v3

--- a/solution.py
+++ b/solution.py
@@ -23,7 +23,9 @@
 HALF = VEC // 2
 PLANES = 2 * ROWS
 KEPT = 22
-LAST = 20
+LAST = 18
+ALONG = LAST + 4
+THIN = 16
 SPARE = 128 - NORB
 PIECES = 5
 
@@ -34,9 +36,9 @@
 
 def kernel(
     chol_ref, green_ref, screen_ref, out_ref,
-    loaded, send, send_last, send_over, recv, recv_last, recv_over, bank, extra, flat, image, rhs, weights, perm, total, mine,
+    loaded, first, first_along, send, send_last, send_over, recv, recv_last, recv_over, bank, extra, flat, image, rhs, weights, perm, total, mine,
     green_mine, green_all, half_in, piece, gathered, result, result_in,
-    load_sem, ready, gather_send, gather_recv, shift_send, shift_recv, swap_send, swap_recv,
+    load_sem, first_sem, ready, gather_send, gather_recv, shift_send, shift_recv, swap_send, swap_recv,
     pair_send, pair_recv, last_send, last_recv, over_send, over_recv, half_send, half_recv, piece_send, piece_recv, out_send, out_recv,
 ):
     k = lax.axis_index("ka")
@@ -53,14 +55,15 @@
         y = lax.rem(lax.rem(me, 4) + dy, 4)
         return x * 4 + y
 
+    def place(group):
+        q = lax.div(group, PER_Q)
+        return q, pl.multiple_of(lax.rem(group, PER_Q) * VEC, VEC)
+
     def load(q):
         return pltpu.make_async_copy(chol_ref.at[q], loaded.at[q], load_sem.at[q])
 
     def wait_bytes(ref, sem):
         pltpu.make_async_copy(ref, ref, sem).wait()
-
-    for q in range(2):
-        load(q).start()
 
     barrier = pltpu.get_barrier_semaphore()
 
@@ -80,31 +83,68 @@
         greet(near_from)
         greet(far)
 
+    for d in range(ORB):
+        q, at = place(peer(d) * SLOTS)
+        pltpu.make_async_copy(
+            chol_ref.at[q, :, :, pl.ds(at, VEC), :], first.at[d], first_sem.at[0]).start()
+        q, at = place(peer(d) * SLOTS + WHOLE)
+        pltpu.make_async_copy(
+            chol_ref.at[q, 1, pl.ds(ALONG - ROWS, 4), pl.ds(at, VEC), :], first_along.at[d],
+            first_sem.at[1]).start()
+
     lane = lax.broadcasted_iota(jnp.int32, (VEC, 128), 1)
 
     def plane_of(group):
-        q = lax.div(group, PER_Q)
-        at = pl.multiple_of(lax.rem(group, PER_Q) * VEC, VEC)
+        q, at = place(group)
 
         def plane(f):
             return pad_lanes(loaded[q, f // ROWS, f % ROWS, pl.ds(at, VEC), :].astype(F32))
 
         return plane
 
-    def fold(plane, kept, put):
+    def along_of(group):
+        q, at = place(group)
+
+        def plane(n):
+            return pad_lanes(loaded[q, 1, ALONG - ROWS + n, pl.ds(at, VEC), :].astype(F32))
+
+        return plane
+
+    def fold(plane, put, thin=None):
         for e in range(4):
-            riding = plane(kept + e)
+            riding = plane(KEPT + e)
             for p in range(PIECES):
                 f = PIECES * e + p
                 moved = pltpu.roll(riding, (NORB - SPARE * p) % 128, 1)
-                put(f, jnp.where(lane < NORB, plane(f), moved))
-
-    def fold_slot(slot, to, put):
-        plane, plane_last = plane_of(to * SLOTS + slot), plane_of(to * SLOTS + WHOLE)
-        fold(plane, KEPT, put)
+                value = jnp.where(lane < NORB, plane(f), moved)
+                if p == PIECES - 1 and thin is not None:
+                    value = jnp.where(lane < 128 - THIN, value, thin(e))
+                put(f, value)
+
+    def fold_slot(slot, plane, along, put):
+        def thin(e):
+            number = 4 * slot + e
+            which = jnp.where(number < 7, 0, 1)
+            piece_at = lax.rem(number, 7)
+            return pltpu.roll(along(which), lax.rem(128 + 128 - THIN - THIN * piece_at, 128), 1)
+
+        fold(plane, put, thin)
         for e in range(2):
-            moved = pltpu.roll(plane_last(LAST + 4 + e), NORB - SPARE * slot, 1)
-            put(LAST + e, jnp.where(lane < NORB, plane(LAST + e), moved))
+            f = PIECES * 4 + e
+            moved = pltpu.roll(along(2 + e), NORB - SPARE * slot, 1)
+            put(f, jnp.where(lane < NORB, plane(f), moved))
+
+    def fold_tail(plane, put):
+        riders = [plane(LAST + e) for e in range(4)]
+        for e in range(4):
+            for p in range(4):
+                moved = pltpu.roll(riders[e], (NORB - SPARE * p) % 128, 1)
+                put(4 * e + p, jnp.where(lane < NORB, plane(4 * e + p), moved))
+        value = plane(16)
+        for e in range(3):
+            value = jnp.where(lane < NORB + 8 * e, value, pltpu.roll(riders[e], 8 + 8 * e, 1))
+        put(16, value)
+        put(17, jnp.where(lane < NORB, plane(17), pltpu.roll(riders[3], 8, 1)))
 
     def halves(put):
         held = {}
@@ -119,14 +159,22 @@
 
         return put_plane
 
-    def send_slot(slot, _):
-        def send_one(d, _):
+    def send_slot(slot, _, early=False):
+        def sources(d):
+            if early:
+                return (lambda f: pad_lanes(first[d, f // ROWS, f % ROWS].astype(F32)),
+                        lambda n: pad_lanes(first_along[d, n].astype(F32)))
+            group = peer(d) * SLOTS
+            return plane_of(group + slot), along_of(group + WHOLE)
+
+        def send_one(n, _):
+            d = ORB - n
             to = peer(d)
 
             def put(f, value):
                 send[slot, d, f] = value.astype(BF16)
 
-            fold_slot(slot, to, put)
+            fold_slot(slot, *sources(d), put)
             pltpu.make_async_remote_copy(
                 src_ref=send.at[slot, d], dst_ref=recv.at[slot, me], send_sem=pair_send.at[slot],
                 recv_sem=pair_recv.at[slot], device_id=(k, core, to), device_id_type=MESH).start()
@@ -137,11 +185,13 @@
         def put_own(f, value):
             recv[slot, me, f] = value.astype(BF16)
 
-        fold_slot(slot, me, put_own)
+        fold_slot(slot, *sources(0), put_own)
         return 0
 
+    wait_bytes(first, first_sem.at[0])
+    wait_bytes(first_along, first_sem.at[1])
     for q in range(2):
-        load(q).wait()
+        load(q).start()
 
     @pl.when(core == 0)
     def _():
@@ -156,7 +206,7 @@
                 src_ref=green_ref, dst_ref=green_mine.at[me], send_sem=gather_send,
                 recv_sem=gather_recv, device_id=(k, core, peer(d)), device_id_type=MESH).start()
 
-    send_slot(0, 0)
+    send_slot(0, 0, early=True)
 
     row = lax.broadcasted_iota(jnp.int32, (256, 256), 0)
     col = lax.broadcasted_iota(jnp.int32, (256, 256), 1)
@@ -167,6 +217,8 @@
     total[...] = jnp.zeros_like(total)
     weights[...] = jnp.zeros_like(weights)
 
+    for q in range(2):
+        load(q).wait()
     send_slot(1, 0)
 
     @pl.when(core == 1)
@@ -188,8 +240,8 @@
             send_over[2 * number + h, n] = value
 
         put = halves(put_over)
-        fold(plane, KEPT, put)
-        for f in range(LAST, KEPT):
+        fold(plane, put)
+        for f in range(PIECES * 4, KEPT):
             put(f, plane(f))
     for number in range(4):
         to = 2 * number + lax.rem(core + number // 2, 2)
@@ -208,11 +260,12 @@
         def put_last(h, n, value):
             send_last[h, d, n] = value
 
-        fold(plane_of(peer(d) * SLOTS + WHOLE), LAST, halves(put_last))
+        fold_tail(plane_of(peer(d) * SLOTS + WHOLE), halves(put_last))
         return 0
 
     def send_last_half(h):
-        def send_one(d, _):
+        def send_one(n, _):
+            d = ORB - n
             pltpu.make_async_remote_copy(
                 src_ref=send_last.at[h, d], dst_ref=recv_last.at[h, me], send_sem=last_send.at[h],
                 recv_sem=last_recv.at[h], device_id=(k, core, peer(d)), device_id_type=MESH).start()
@@ -256,13 +309,23 @@
         src_ref=total.at[pl.ds(pl.multiple_of(other * half, half), half)], dst_ref=half_in,
         send_sem=half_send, recv_sem=half_recv, device_id=(k, other, me), device_id_type=MESH)
 
-    def unfold(planes, kept, o, put):
+    def pieced(pieces):
+        for n, (tile, by, start) in enumerate(pieces):
+            back = pltpu.roll(tile.astype(F32), by, 1)
+            value = jnp.where(lane >= start, back, value) if n else back
+        return value
+
+    def unfold(planes, put):
         for e in range(4):
-            for p in range(PIECES):
-                carrier = planes(PIECES * e + p).astype(F32)
-                back = pltpu.roll(carrier, SPARE + SPARE * p, 1)
-                value = jnp.where(lane >= SPARE * p, back, value) if p else back
-            put(e, value.astype(BF16))
+            put(e, pieced([
+                (planes(PIECES * e + p), SPARE + SPARE * p, SPARE * p) for p in range(PIECES)
+            ]).astype(BF16))
+
+    def unfold_tail(planes, put):
+        for e in range(4):
+            pieces = [(planes(4 * e + p), SPARE + SPARE * p, SPARE * p) for p in range(4)]
+            pieces.append((planes(16), 120 - 8 * e, 96) if e < 3 else (planes(17), 120, 96))
+            put(e, pieced(pieces).astype(BF16))
 
     def turn(plane, vectors):
         for jb in range(PADDED // 16):
@@ -302,7 +365,7 @@
             def put(e, value, o=o):
                 extra[o, e] = value
 
-            unfold(lambda f, o=o: recv[slot, o, f], KEPT, o, put)
+            unfold(lambda f, o=o: recv[slot, o, f], put)
         turn(lambda o, f: recv[slot, o, f] if f < KEPT else extra[o, f - KEPT], VEC)
         image_of(lax.div(group, PER_Q), lax.rem(group, PER_Q) * VEC, VEC)
         add(slice(None), VEC)
@@ -311,7 +374,7 @@
     def turned_over(value):
         return jnp.concatenate([value[HALF:], value[:HALF]], axis=0)
 
-    def unpack(tiles, kept):
+    def unpack(tiles, kept, spread):
         for o in range(ORB):
             for n in range(kept // 2):
                 tile = tiles(o, n)
@@ -321,7 +384,15 @@
             def put(e, value, o=o):
                 bank[o, kept + e] = value
 
-            unfold(lambda f, o=o: bank[o, f], kept, o, put)
+            spread(lambda f, o=o: bank[o, f], put)
+
+    def along_planes(o):
+        for a in range(2):
+            pieces = [divmod(7 * a + m, 4) for m in range(7)]
+            yield pieced([(recv[p, o, PIECES * e + 4], THIN + THIN * m, THIN * m)
+                          for m, (p, e) in enumerate(pieces)])
+        for e in range(2):
+            yield pieced([(recv[p, o, 20 + e], SPARE + SPARE * p, SPARE * p) for p in range(WHOLE)])
 
     def work_half(position, _):
         h = jnp.where(position == 0, lax.rem(over_at, 2), position - 1)
@@ -330,18 +401,15 @@
         @pl.when(position == 0)
         def _():
             wait_bytes(recv_over.at[pl.ds(0, ORB - 1)], over_recv)
-            unpack(lambda o, n: recv_over[o, n], KEPT)
+            unpack(lambda o, n: recv_over[o, n], KEPT, unfold)
 
         @pl.when(position != 0)
         def _():
+            for o in range(ORB):
+                for n, value in enumerate(along_planes(o)):
+                    bank[o, ALONG + n] = jnp.where(h == 1, turned_over(value), value).astype(BF16)
             wait_bytes(recv_last.at[h, pl.ds(0, ORB - 1)], last_recv.at[h])
-            unpack(lambda o, n: recv_last[h, o, n], LAST)
-            for o in range(ORB):
-                for e in range(2):
-                    for p in range(PIECES):
-                        back = pltpu.roll(recv[p, o, LAST + e].astype(F32), SPARE + SPARE * p, 1)
-                        value = jnp.where(lane >= SPARE * p, back, value) if p else back
-                    bank[o, LAST + 4 + e] = jnp.where(h == 1, turned_over(value), value).astype(BF16)
+            unpack(lambda o, n: recv_last[h, o, n], LAST, unfold_tail)
 
         turn(lambda o, f: bank[o, f], HALF)
         image_of(lax.div(group, PER_Q), lax.rem(group, PER_Q) * VEC + HALF * h, HALF)
@@ -438,6 +506,8 @@
         out_specs=pl.BlockSpec(memory_space=pltpu.VMEM),
         scratch_shapes=[
             pltpu.VMEM((2, 2, ROWS, PER_Q * VEC, NORB), BF16),
+            pltpu.VMEM((ORB, 2, ROWS, VEC, NORB), BF16),
+            pltpu.VMEM((ORB, 4, VEC, NORB), BF16),
             pltpu.VMEM((WHOLE, ORB, KEPT, VEC, 128), BF16),
             pltpu.VMEM((2, ORB, LAST // 2, VEC, 128), BF16),
             pltpu.VMEM((4, KEPT // 2, VEC, 128), BF16),
@@ -460,7 +530,7 @@
             pltpu.VMEM((ORB, 56, 128), F32),
             pltpu.VMEM((56, 128), F32),
             pltpu.VMEM((56, 128), F32),
-            dma((2,)), pltpu.SemaphoreType.REGULAR, dma, dma, dma((2,)), dma((2,)), dma, dma,
+            dma((2,)), dma((2,)), pltpu.SemaphoreType.REGULAR, dma, dma, dma((2,)), dma((2,)), dma, dma,
             dma((WHOLE,)), dma((WHOLE,)), dma((2,)), dma((2,)), dma, dma,
             dma, dma, dma, dma, dma, dma,
         ],

time: 69.1 us -> 68.1 us (0.986)
  Pallas kernels: 68.3 us -> 67.2 us
    pallas_call x1, Pallas kernels: 68.3 us -> 67.2 us  [body(): pl.pallas_call(kernel, out_shape=pltpu.VMEM((TAUS, ROWS, 2, NORB), F32),...]
where the time goes in v4:
time: 68.1 us; the launch traced here: 67.9 us
  Pallas kernels  67.2 us (99%)
    pallas_call x1, Pallas kernels, body(): pl.pallas_call(kernel, out_shape=pltpu.VMEM((TAUS, ROWS, 2, NORB), F32),...  67.2 us

profile of v4, /device:TPU:1, one launch (start us, length us, event | category | flops | bytes accessed | tf_op | source)
XLA Modules:
  0.0 67.9 jit_solution(63135983914098334)
XLA Ops:
  0.0 67.2 %shard_map.37 = f32[4,13,2,104]{3,2,1,0:T(2,128)S(1)} custom-call(bf16[2,2,13,400,104]{4,3,2,1,0:T(8,128)(2,1)} %bitcast.10, bf16[4,13,2,104]{3,2,1,0:T(2,128)(2,1)} %bitcast.11, f32[2,4,400]{2,1,0:T(4,128)} %screen_ref.1), custom_call_target="tpu_custom_call" | custom-call | flops 7200000000 | bytes 5400000 | tf_op jit(solution)/shard_map/pallas_call | solution.py:498
  67.2 0.6 copy.5

commit v5 on v4

--- a/solution.py
+++ b/solution.py
@@ -37,7 +37,7 @@
 def kernel(
     chol_ref, green_ref, screen_ref, out_ref,
     loaded, first, first_along, send, send_last, send_over, recv, recv_last, recv_over, bank, extra, flat, image, rhs, weights, perm, total, mine,
-    green_mine, green_all, half_in, piece, gathered, result, result_in,
+    green_mine, green_all, half_in, cut, piece, gathered, result, result_in,
     load_sem, first_sem, ready, gather_send, gather_recv, shift_send, shift_recv, swap_send, swap_recv,
     pair_send, pair_recv, last_send, last_recv, over_send, over_recv, half_send, half_recv, piece_send, piece_recv, out_send, out_recv,
 ):
@@ -439,16 +439,17 @@
             rows = pltpu.roll(around, 24 - (ROWS * to - base), 0)[0:ROWS]
             for ri in range(2):
                 at = ROWS * (2 * t + ri)
-                piece[d, at:at + ROWS] = rows[:, 128 * ri:128 * ri + 128]
+                cut[d, at:at + ROWS] = rows[:, 128 * ri:128 * ri + 128]
         if d:
+            piece[d] = cut[d].astype(BF16)
             pltpu.make_async_remote_copy(
                 src_ref=piece.at[d], dst_ref=gathered.at[me], send_sem=piece_send,
                 recv_sem=piece_recv, device_id=(k, core, to), device_id_type=MESH).start()
-    gathered[me] = piece[0]
+    gathered[me] = jnp.zeros_like(piece[0])
     wait_bytes(gathered.at[pl.ds(0, ORB - 1)], piece_recv)
-    summed = gathered[0]
-    for o in range(1, ORB):
-        summed = summed + gathered[o]
+    summed = cut[0]
+    for o in range(ORB):
+        summed = summed + gathered[o].astype(F32)
     result[...] = summed
     hand_over = pltpu.make_async_remote_copy(
         src_ref=result, dst_ref=result_in, send_sem=out_send, recv_sem=out_recv,
@@ -526,10 +527,11 @@
             pltpu.VMEM((ORB, TAUS, ROWS, 2, NORB), BF16),
             pltpu.VMEM((2, ORB, TAUS, ROWS, 2, NORB), BF16),
             pltpu.VMEM((2 * PADDED, 256), F32),
-            pltpu.VMEM((ORB, 56, 128), F32),
-            pltpu.VMEM((ORB, 56, 128), F32),
-            pltpu.VMEM((56, 128), F32),
-            pltpu.VMEM((56, 128), F32),
+            pltpu.VMEM((ORB, 64, 128), F32),
+            pltpu.VMEM((ORB, 64, 128), BF16),
+            pltpu.VMEM((ORB, 64, 128), BF16),
+            pltpu.VMEM((64, 128), F32),
+            pltpu.VMEM((64, 128), F32),
             dma((2,)), dma((2,)), pltpu.SemaphoreType.REGULAR, dma, dma, dma((2,)), dma((2,)), dma, dma,
             dma((WHOLE,)), dma((WHOLE,)), dma((2,)), dma((2,)), dma, dma,
             dma, dma, dma, dma, dma, dma,

time: 68.1 us -> 67 us (0.984)
  Pallas kernels: 67.2 us -> 66.2 us
    pallas_call x1, Pallas kernels: 67.2 us -> 66.2 us  [body(): pl.pallas_call(kernel, out_shape=pltpu.VMEM((TAUS, ROWS, 2, NORB), F32),...]
where the time goes in v5:
time: 67 us; the launch traced here: 66.8 us
  Pallas kernels  66.2 us (99%)
    pallas_call x1, Pallas kernels, body(): pl.pallas_call(kernel, out_shape=pltpu.VMEM((TAUS, ROWS, 2, NORB), F32),...  66.2 us

profile of v5, /device:TPU:1, one launch (start us, length us, event | category | flops | bytes accessed | tf_op | source)
XLA Modules:
  0.0 66.8 jit_solution(8413090832088956860)
XLA Ops:
  0.0 66.2 %shard_map.37 = f32[4,13,2,104]{3,2,1,0:T(2,128)S(1)} custom-call(bf16[2,2,13,400,104]{4,3,2,1,0:T(8,128)(2,1)} %bitcast.10, bf16[4,13,2,104]{3,2,1,0:T(2,128)(2,1)} %bitcast.11, f32[2,4,400]{2,1,0:T(4,128)} %screen_ref.1), custom_call_target="tpu_custom_call" | custom-call | flops 7200000000 | bytes 5400000 | tf_op jit(solution)/shard_map/pallas_call | solution.py:499
  66.2 0.6 copy.5

commit v6 on v5

--- a/solution.py
+++ b/solution.py
@@ -36,7 +36,7 @@
 
 def kernel(
     chol_ref, green_ref, screen_ref, out_ref,
-    loaded, first, first_along, send, send_last, send_over, recv, recv_last, recv_over, bank, extra, flat, image, rhs, weights, perm, total, mine,
+    loaded, first, first_along, send, send_last, send_over, recv, recv_last, recv_over, bank, extra, flat, image, rhs, weights, perm, total,
     green_mine, green_all, half_in, cut, piece, gathered, result, result_in,
     load_sem, first_sem, ready, gather_send, gather_recv, shift_send, shift_recv, swap_send, swap_recv,
     pair_send, pair_recv, last_send, last_recv, over_send, over_recv, half_send, half_recv, piece_send, piece_recv, out_send, out_recv,
@@ -429,14 +429,14 @@
     lax.fori_loop(0, WHOLE, work_whole, 0)
     lax.fori_loop(jnp.where(has_over, 0, 1), 3, work_half, 0)
 
-    swap_half.wait()
-    mine[...] = -(total[pl.ds(pl.multiple_of(core * half, half), half), :] + half_in[...])
+    swap_half.wait_recv()
     for d in (4, 5, 7, 6, 1, 3, 2, 0):
         to = peer(d)
         for t in range(2):
             base = pl.multiple_of(lax.div(ROWS * to, 8) * 8, 8)
-            around = mine[pl.ds(t * PADDED + base, 24), :]
-            rows = pltpu.roll(around, 24 - (ROWS * to - base), 0)[0:ROWS]
+            here = pl.multiple_of(core * half + t * PADDED + base, 8)
+            around = total[pl.ds(here, 24), :] + half_in[pl.ds(t * PADDED + base, 24), :]
+            rows = -pltpu.roll(around, 24 - (ROWS * to - base), 0)[0:ROWS]
             for ri in range(2):
                 at = ROWS * (2 * t + ri)
                 cut[d, at:at + ROWS] = rows[:, 128 * ri:128 * ri + 128]
@@ -464,6 +464,7 @@
 
     put_out(core, result)
 
+    swap_half.wait_send()
     wait_bytes(piece.at[pl.ds(0, ORB - 1)], piece_send)
 
     def sent_slot(slot, _):
@@ -523,7 +524,6 @@
             pltpu.VMEM((2, 256, TAUS * 256), BF16),
             pltpu.VMEM((256, 256), BF16),
             pltpu.VMEM((TAUS * PADDED, 256), F32),
-            pltpu.VMEM((2 * PADDED, 256), F32),
             pltpu.VMEM((ORB, TAUS, ROWS, 2, NORB), BF16),
             pltpu.VMEM((2, ORB, TAUS, ROWS, 2, NORB), BF16),
             pltpu.VMEM((2 * PADDED, 256), F32),

time: 67 us -> 66.9 us (level)
  no operation moved by 1% of the time
where the time goes in v6:
time: 66.9 us; the launch traced here: 66.7 us
  Pallas kernels  66 us (99%)
    pallas_call x1, Pallas kernels, body(): pl.pallas_call(kernel, out_shape=pltpu.VMEM((TAUS, ROWS, 2, NORB), F32),...  66 us

profile of v6, /device:TPU:1, one launch (start us, length us, event | category | flops | bytes accessed | tf_op | source)
XLA Modules:
  0.0 66.7 jit_solution(5032482851542588416)
XLA Ops:
  0.0 66.0 %shard_map.37 = f32[4,13,2,104]{3,2,1,0:T(2,128)S(1)} custom-call(bf16[2,2,13,400,104]{4,3,2,1,0:T(8,128)(2,1)} %bitcast.10, bf16[4,13,2,104]{3,2,1,0:T(2,128)(2,1)} %bitcast.11, f32[2,4,400]{2,1,0:T(4,128)} %screen_ref.1), custom_call_target="tpu_custom_call" | custom-call | flops 7200000000 | bytes 5400000 | tf_op jit(solution)/shard_map/pallas_call | solution.py:500
  66.0 0.6 copy.5
